TPU v7x, 512 devices: a whole 4x8x8 slice. The times are simulated.
512 devices in a mesh: rank: 8 (over z_hi, x), fsdp: 64 (over y, z_lo, core).
Axes of the slice: x: 4, y: 8, z: 8 (z_hi: 2, z_lo: 4; z = z_hi * 4 + z_lo), core: 2. Of those that a mesh axis runs over, the one named last changes fastest.
Arguments:
- cotangents: bfloat16 [8192, 8192], P('fsdp', 'rank'), may hold values from -0.25 to 0.25
- hidden: bfloat16 [8192, 14336], P('fsdp'), may hold values from -6 to 6
- projector: bfloat16 [8192, 2048], P('rank', 'fsdp'), may hold values from -0.0625 to 0.0625
- moment_first: bfloat16 [2048, 14336], P('rank', 'fsdp'), may hold values from -3 to 3
- moment_second: bfloat16 [2048, 14336], P('rank', 'fsdp'), may hold values from 0.0039978027 to 0.3984375
Outputs:
- update: bfloat16 [8192, 14336], P('rank', 'fsdp')
- first_moment: bfloat16 [2048, 14336], P('rank', 'fsdp')
- second_moment: bfloat16 [2048, 14336], P('rank', 'fsdp')
All inputs are finite; a program needn't handle non-finite values.
Results may differ from a plain program's by a relative error of at most 0.019.
Values may be sent and summed in bfloat16 or wider, within the bound.
A program may use at most 64 MiB of HBM per device.

v0:
```python
import jax
import jax.numpy as jnp
from jax import lax
from jax.sharding import PartitionSpec as P

STEP = 20


def per_device(cotangents, hidden, projector, moment_first, moment_second):
    proj_rows = lax.all_gather(projector, "fsdp", axis=1, tiled=True)
    columns = proj_rows
    left_local = lax.psum_scatter(
        lax.dot_general(
            columns, cotangents, (((0,), (1,)), ((), ())), preferred_element_type=jnp.float32
        ).astype(jnp.bfloat16),
        "rank",
        scatter_dimension=0,
        tiled=True,
    )
    hidden_cols = lax.all_to_all(hidden, "fsdp", split_axis=1, concat_axis=0, tiled=True)
    projected = jnp.dot(
        lax.all_gather(left_local, "fsdp", axis=1, tiled=True),
        hidden_cols,
        preferred_element_type=jnp.float32,
    )
    first_f = 0.9 * moment_first.astype(jnp.float32) + 0.1 * projected
    second_f = 0.999 * moment_second.astype(jnp.float32) + 0.001 * projected * projected
    first_fix = 1.0 - 0.9**STEP
    second_fix = 1.0 - 0.999**STEP
    direction = (first_f / first_fix / (jnp.sqrt(second_f / second_fix) + 1e-08)).astype(
        jnp.bfloat16
    )
    columns = proj_rows
    update = jnp.dot(
        columns,
        lax.all_gather(direction, "rank", axis=0, tiled=True),
        preferred_element_type=jnp.float32,
    )
    return (
        update.astype(jnp.bfloat16),
        first_f.astype(jnp.bfloat16),
        second_f.astype(jnp.bfloat16),
    )


def solution(mesh):
    return jax.shard_map(
        per_device,
        mesh=mesh,
        in_specs=(
            P("fsdp", "rank"),
            P("fsdp", None),
            P("rank", "fsdp"),
            P("rank", "fsdp"),
            P("rank", "fsdp"),
        ),
        out_specs=(P("rank", "fsdp"), P("rank", "fsdp"), P("rank", "fsdp")),
        check_vma=False,
    )
```

profile of v0, /device:TPU:1, one launch (start us, length us, event | category | flops | bytes accessed | tf_op | source)
XLA Modules:
  0.0 469.4 jit_solution(1852249544239048835)
XLA Ops:
  7.2 0.0 copy-start
  7.2 0.0 all-gather.3.cloned.1.call-start
  7.2 0.7 all-gather.3.cloned.1.call-update
  7.9 0.0 reduce-scatter.2.cloned.1.call-start
  8.0 128.7 %all-gather.3.cloned.1.call-done = bf16[1024,2048]{0,1:T(8,128)(2,1)} async-done(((bf16[1024,32]{0,1:T(8,128)(2,1)}), bf16[1024,2048]{0,1:T(8,128)(2,1)}) %all-gather.3.cloned.1.call-update) | async-done | bytes 4194320 | tf_op jit(solution)/shard_map/all_gather | solution.py:10
  136.6 0.0 copy-done
  136.6 4.2 convolution_convert_fusion
  140.9 0.0 reduce-scatter.2.cloned.1.call-update
  140.9 0.0 all-gather.5.cloned.1.call-start
  140.9 85.5 %reduce-scatter.2.cloned.1.call-done = bf16[256,128]{1,0:T(8,128)(2,1)} async-done(((bf16[2048,128]{1,0:T(8,128)(2,1)}), bf16[256,128]{1,0:T(8,128)(2,1)}) %reduce-scatter.2.cloned.1.call-update) | async-done | bytes 65552 | tf_op jit(solution)/shard_map/reduce_scatter | solution.py:12
  226.4 0.0 all-gather.5.cloned.1.call-update
  226.5 6.0 %copy.8 = bf16[128,14336]{0,1:T(8,128)(2,1)} copy(bf16[128,14336]{1,0:T(8,128)(2,1)} %param.6) | data formatting | bytes 7340032 | tf_op args[1]
  232.5 0.0 copy-start.2
  232.5 0.0 copy-start.3
  232.5 101.6 %all_to_all.19 = bf16[128,64,224]{0,2,1:T(8,128)(2,1)} all-to-all(bf16[128,64,224]{0,2,1:T(8,128)(2,1)} %bitcast.18), channel_id=1, replica_groups=mesh['rank'=8,'fsdp'=64] {'fsdp'}, dimensions={1} | all-to-all | bytes 7340032 | tf_op jit(solution)/shard_map/all_to_all | solution.py:20
  334.2 79.0 %all-gather.5.cloned.1.call-done = bf16[256,8192]{1,0:T(8,128)(2,1)} async-done(((bf16[256,128]{1,0:T(8,128)(2,1)}), bf16[256,8192]{1,0:T(8,128)(2,1)}) %all-gather.5.cloned.1.call-update) | async-done | bytes 4194320 | tf_op jit(solution)/shard_map/all_gather | solution.py:22
  413.2 0.0 copy-done.2
  413.2 0.0 copy-done.3
  413.2 0.0 copy-start.1
  413.2 5.6 %fusion.6 = (bf16[256,224]{0,1:T(8,128)(2,1)}, bf16[256,224]{0,1:T(8,128)(2,1)S(1)}, bf16[256,224]{0,1:T(8,128)(2,1)}) fusion(bf16[256,224]{0,1:T(8,128)(2,1)S(1)} %copy-done.2, bf16[256,224]{0,1:T(8,128)(2,1)S(1)} %copy-done.3, bf16[256,8192]{1,0:T(8,128)(2,1)} %all-gather.5.cloned.1.call-done, bf16[128,64,224]{0,2,1:T(8,128)(2,1)} %all_to_all.19), kind=kOutput, calls=%fused_computation.11 | convolution fusion | flops 940441600 | bytes 8437760 | tf_op jit(solution)/shard_map/dot_general | solution.py:21
  418.8 42.1 %all_gather.11 = bf16[2048,224]{0,1:T(8,128)(2,1)S(1)} all-gather(bf16[256,224]{0,1:T(8,128)(2,1)S(1)} %get-tuple-element.4), channel_id=1, replica_groups=mesh['rank'=8,'fsdp'=64] {'rank'}, dimensions={0}, use_global_device_ids=true | all-gather | bytes 1032192 | tf_op jit(solution)/shard_map/all_gather | solution.py:36
  460.9 0.0 copy-done.1
  460.9 1.9 fusion.3
Async XLA Ops:
  7.2 129.5 %copy-start = (bf16[128,1024]{1,0:T(8,128)(2,1)S(1)}, bf16[128,1024]{1,0:T(8,128)(2,1)}, u32[]{:S(2)}) copy-start(bf16[128,1024]{1,0:T(8,128)(2,1)} %param.5) | copy-start | bytes 786436
  7.2 129.4 %all-gather.3.cloned.1.call-start = ((), (), s32[]{:S(2)}) async-start(), calls=%async_computation.2 | async-start | bytes 4259840 | tf_op jit(solution)/shard_map/all_gather | solution.py:10
  7.9 218.5 %reduce-scatter.2.cloned.1.call-start = ((), (), s32[]{:S(2)}) async-start(), calls=%async_computation.3 | async-start | bytes 589824 | tf_op jit(solution)/shard_map/reduce_scatter | solution.py:12
  140.9 272.3 %all-gather.5.cloned.1.call-start = ((), (), s32[]{:S(2)}) async-start(), calls=%async_computation.4 | async-start | bytes 4259840 | tf_op jit(solution)/shard_map/all_gather | solution.py:22
  232.5 180.7 %copy-start.2 = (bf16[256,224]{0,1:T(8,128)(2,1)S(1)}, bf16[256,224]{0,1:T(8,128)(2,1)}, u32[]{:S(2)}) copy-start(bf16[256,224]{0,1:T(8,128)(2,1)} %param.9) | copy-start | bytes 344068
  232.5 180.7 %copy-start.3 = (bf16[256,224]{0,1:T(8,128)(2,1)S(1)}, bf16[256,224]{0,1:T(8,128)(2,1)}, u32[]{:S(2)}) copy-start(bf16[256,224]{0,1:T(8,128)(2,1)} %param.8) | copy-start | bytes 344068
  413.2 47.7 %copy-start.1 = (bf16[1024,2048]{0,1:T(8,128)(2,1)S(1)}, bf16[1024,2048]{0,1:T(8,128)(2,1)}, u32[]{:S(2)}) copy-start(bf16[1024,2048]{0,1:T(8,128)(2,1)} %all-gather.3.cloned.1.call-done) | copy-start | bytes 12582916
Sparse Core Ops, SparseCore 0:
  10.2 126.4 all-gather.2
  141.1 85.3 reduce-scatter.1
  228.7 184.4 all-gather.4
where the time goes:
time: 473 us; the launch traced here: 469 us
  waiting for transfers between devices  294 us (62%)
  blocking collectives  144 us (30%)
  between operations  13.8 us (3%)
  matrix products  11.8 us (2%)
  local copies, waits for them, and re-layouts  6.06 us (1%)
    all_gather x1, waiting for transfers between devices, per_device(): proj_rows = lax.all_gather(projector, 'fsdp', axis=1, tiled=True)  129 us
    all_to_all x1, blocking collectives, per_device(): lax.all_to_all(hidden, 'fsdp', split_axis=1, concat_axis=0, tiled=True)  102 us
    reduce_scatter x1, waiting for transfers between devices, per_device(): lax.psum_scatter(lax.dot_general(columns, cotangents, (((0,), (1,)), ((),...  85.5 us
    all_gather x1, waiting for transfers between devices, per_device(): lax.all_gather(left_local, 'fsdp', axis=1, tiled=True)  79 us
    all_gather x1, blocking collectives, per_device(): lax.all_gather(direction, 'rank', axis=0, tiled=True)  42.1 us
  transfers between devices with their start and end apart: 3, of which 3 were waited for; matrix products, arithmetic and copies ran while one was open for 1% of the time, Pallas kernels for 0%

commit v1 on v0

v1 whole, which is shorter than its diff:
```python
import jax
import jax.numpy as jnp
from jax import lax
from jax.experimental import pallas as pl
from jax.experimental.pallas import tpu as pltpu
from jax.sharding import PartitionSpec as P

STEP = 20
FIRST_FIX = 1.0 - 0.9**STEP
SECOND_FIX = 1.0 - 0.999**STEP
BF = jnp.bfloat16
F32 = jnp.float32
MESH = pl.DeviceIdType.MESH
ORDER = (4, 3, 5, 2, 6, 1, 7, 0)
OWNER = {4: (0, 0), 3: (0, 1), 5: (0, 2), 2: (0, 3), 0: (1, 0), 7: (1, 1), 1: (1, 2), 6: (1, 3)}


def body(
    cot, hid, prj, mom1, mom2,
    upd, new1, new2,
    hid_v, hid_t, hbuf, p_t, cot_t, xs, xb, zs, zb, lt, lt2, part, stage, arrived, dr, m1t, m2t, pad,
    loc_sem,
    pp_s, pp_r, ct_s, ct_r, ring_s, ring_r, hz_s, hz_r, hx_s, hx_r, hs_s, hs_r,
    ls_s, ls_r, lz_s, lz_r, lg_s, lg_r, lc_s, lc_r, p2_s, p2_r, pc_s, pc_r,
    rs_s, rs_r, dz_s, dz_r, dx_s, dx_r,
):
    rank = lax.axis_index("rank")
    shard = lax.axis_index("fsdp")
    zh, x = rank // 4, rank % 4
    y, zl, c = shard // 8, (shard // 2) % 4, shard % 2
    z = zh * 4 + zl
    low, high, pair = zl % 2, zl // 2, zl // 2

    def at(zh_, x_, y_, zl_, c_):
        return (zh_ * 4 + x_, y_ * 8 + zl_ * 2 + c_)

    def at_z(z_, c_):
        return at(z_ // 4, x, y, z_ % 4, c_)

    def rcopy(src, dst, ssem, rsem, dev):
        return pltpu.make_async_remote_copy(
            src_ref=src, dst_ref=dst, send_sem=ssem, recv_sem=rsem, device_id=dev, device_id_type=MESH
        )

    sibling = at(zh, x, y, zl, 1 - c)
    partner = at(1 - zh, x, y, zl, c)
    up, down = at(zh, x, (y + 1) % 8, zl, c), at(zh, x, (y + 7) % 8, zl, c)
    xpeers = [((x + k) % 4, at(zh, (x + k) % 4, y, zl, c)) for k in (1, 2, 3)]
    zpeers = [((zl + k) % 4, at(zh, x, y, (zl + k) % 4, c)) for k in (1, 2, 3)]

    load = pltpu.make_async_copy(hid, hid_v, loc_sem.at[0])
    load.start()

    own_lane = pl.multiple_of(low * 256 + c * 128, 128)
    own_rows = pl.multiple_of(high * 32, 32)
    other_rows = pl.multiple_of((1 - high) * 32, 32)
    p_t[y, low, c, pl.ds(own_rows, 32), :] = prj[...].T
    cot_t[:, pl.ds(own_lane, 128)] = cot[...].T

    barrier = pltpu.get_barrier_semaphore()
    greet = [sibling, partner, up, down] + [d for _, d in xpeers] + [d for _, d in zpeers]
    for off in (1, 7, 2, 6):
        for cc in (0, 1):
            greet.append(at_z((z + off) % 8, cc))
    for dev in greet:
        pl.semaphore_signal(barrier, inc=1, device_id=dev, device_id_type=MESH)
    pl.semaphore_wait(barrier, len(greet))

    sends = []

    pp = rcopy(
        p_t.at[y, low, c, pl.ds(own_rows, 32)], p_t.at[y, low, c, pl.ds(own_rows, 32)],
        pp_s, pp_r, at(zh, x, y, (zl + 2) % 4, c),
    )
    pp.start()
    pp_in = rcopy(
        p_t.at[y, low, c, pl.ds(other_rows, 32)], p_t.at[y, low, c, pl.ds(other_rows, 32)],
        pp_s, pp_r, at(zh, x, y, (zl + 2) % 4, c),
    )

    def ring(direction, h, step, incoming=False):
        back = step + (1 if incoming else 0)
        origin = (y + 8 - back) % 8 if direction == 0 else (y + back) % 8
        rows = pl.multiple_of(h * 32, 32)
        ref = p_t.at[origin, low, c, pl.ds(rows, 32)]
        return rcopy(
            ref, ref, ring_s.at[direction, h, step], ring_r.at[direction, h, step], up if direction == 0 else down
        )

    ring(0, high, 0).start()
    ring(1, high, 0).start()

    ct = [
        rcopy(cot_t.at[:, pl.ds(own_lane, 128)], cot_t.at[:, pl.ds(own_lane, 128)], ct_s.at[0], ct_r.at[0],
              at(zh, x, y, zl + 1 - 2 * low, c)),
        rcopy(cot_t.at[:, pl.ds(own_lane, 128)], cot_t.at[:, pl.ds(own_lane, 128)], ct_s.at[1], ct_r.at[1], sibling),
    ]
    for copy in ct:
        copy.start()

    def transpose_block(block):
        def tile(t, carry):
            column = pl.multiple_of(block * 1792 + t * 128, 128)
            row = pl.multiple_of(t * 128, 128)
            hid_t[block, pl.ds(row, 128), :] = hid_v[:, pl.ds(column, 128)].T
            return carry

        lax.fori_loop(0, 14, tile, 0, unroll=7)

    first = jnp.where(x == 0, 4, jnp.where(x == 1, 3, jnp.where(x == 2, 5, 2)))
    blocks = [(y + first) % 8, (y + first + 4) % 8]

    def hidden_sends(rnd):
        out = []
        block = blocks[rnd]
        for k, (off, rot) in enumerate(((1, 3), (7, 1), (None, 2))):
            zd = (z + off) % 8 if off is not None else (z + 2 + 4 * c) % 8
            lane = pl.multiple_of(rot * 256 + c * 128, 128)
            for cc in (0, 1):
                row = pl.multiple_of((2 * (zd % 4) + cc) * 224, 16)
                out.append(rcopy(
                    hid_t.at[block, pl.ds(row, 224)], hbuf.at[block, :, pl.ds(lane, 128)],
                    hz_s.at[rnd, k, cc], hz_r.at[rnd, 2 * k + c], at_z(zd, cc),
                ))
        return out

    def hidden_wait(rnd):
        block = blocks[rnd]
        for k, rot in enumerate((3, 1, 2)):
            for cc in (0, 1):
                lane = rot * 256 + cc * 128
                ref = hbuf.at[block, :, pl.ds(lane, 128)]
                rcopy(ref, ref, hz_s.at[rnd, k, cc], hz_r.at[rnd, 2 * k + cc], sibling).wait_recv()

    def hidden_forward(rnd):
        ref = hbuf.at[blocks[rnd], :, pl.ds(256, 768)]
        return [
            rcopy(ref, ref, hx_s.at[rnd, k], hx_r.at[rnd, x], dev) for k, (_, dev) in enumerate(xpeers)
        ]

    load.wait()
    hz = []
    for rnd in (0, 1):
        transpose_block(blocks[rnd])
        copies = hidden_sends(rnd)
        for copy in copies:
            copy.start()
        hz += copies

    pp_in.wait_recv()
    ring(0, 1 - high, 0).start()
    ring(1, 1 - high, 0).start()

    other_lane = pl.multiple_of((1 - low) * 256 + c * 128, 128)
    ct_in = rcopy(cot_t.at[:, pl.ds(other_lane, 128)], cot_t.at[:, pl.ds(other_lane, 128)], ct_s.at[0], ct_r.at[0], sibling)
    ct_in.wait_recv()
    ct.append(rcopy(cot_t.at[:, pl.ds(other_lane, 128)], cot_t.at[:, pl.ds(other_lane, 128)], ct_s.at[2], ct_r.at[2], sibling))
    ct[2].start()
    for k, lo in ((1, low), (2, 1 - low)):
        lane = pl.multiple_of(lo * 256 + (1 - c) * 128, 128)
        ref = cot_t.at[:, pl.ds(lane, 128)]
        rcopy(ref, ref, ct_s.at[k], ct_r.at[k], sibling).wait_recv()

    def left_copy(block):
        return rcopy(
            xs.at[block], xb.at[x, block // 4], ls_s.at[block], ls_r.at[x, block // 4], at(zh, block % 4, y, zl, c)
        )

    def left_block(block):
        xs[block] = jnp.dot(p_t[block, low, c], cot_t[...], preferred_element_type=F32).astype(BF)

        @pl.when(block % 4 != x)
        def _():
            left_copy(block).start()

    left_block(y)
    hx = []
    for step in range(4):
        for direction, h in ((0, 0), (1, 1), (0, 1), (1, 0)):
            if step == 3 and direction != h:
                continue
            ring(direction, h, step, incoming=True).wait_recv()
            if step < 2 or (step == 2 and direction == h):
                ring(direction, h, step + 1).start()
        if step < 3:
            left_block((y + 7 - step) % 8)
            left_block((y + 1 + step) % 8)
        else:
            left_block((y + 4) % 8)
        if step == 0:
            for k in range(1, 4):
                transpose_block((blocks[0] + k) % 8)
        if step == 1:
            for k in range(5, 8):
                transpose_block((blocks[0] + k) % 8)
            hidden_wait(0)
            copies = hidden_forward(0)
            for copy in copies:
                copy.start()
            hx += copies
        if step == 2:
            own = pltpu.make_async_copy(
                hid_t.at[:, pl.ds(pl.multiple_of((2 * zl + c) * 224, 16), 224)],
                hbuf.at[:, :, pl.ds(pl.multiple_of(c * 128, 128), 128)],
                loc_sem.at[1],
            )
            own.start()
            hs = rcopy(
                hid_t.at[:, pl.ds(pl.multiple_of((2 * zl + 1 - c) * 224, 16), 224)],
                hbuf.at[:, :, pl.ds(pl.multiple_of(c * 128, 128), 128)],
                hs_s, hs_r, sibling,
            )
            hs.start()

    def left_wait(half):
        for sx, _ in xpeers:
            ref = xb.at[sx, half]
            rcopy(ref, ref, ls_s.at[0], ls_r.at[sx, half], sibling).wait_recv()

    def left_sum(half):
        total = xs[half * 4 + x].astype(F32)
        for sx, _ in xpeers:
            total = total + xb[sx, half].astype(F32)
        return total

    left_wait(1 - zh)
    zs[...] = left_sum(1 - zh).astype(BF)
    lz = rcopy(zs, zb, lz_s, lz_r, partner)
    lz.start()
    hidden_wait(1)
    copies = hidden_forward(1)
    for copy in copies:
        copy.start()
    hx += copies
    for src, dst in ((mom1, m1t), (mom2, m2t)):
        pad[...] = jnp.zeros_like(pad)
        pad[:, :224] = src[...].astype(F32)
        dst[...] = pad[...].T[:224, :]
    left_wait(zh)
    lz.wait_recv()
    lt[pair, low, c] = (left_sum(zh) + zb[...].astype(F32)).astype(BF)

    mine = lt.at[pair, low, c]
    lg = [rcopy(mine, mine, lg_s.at[k], lg_r.at[zl], dev) for k, (_, dev) in enumerate(zpeers)]
    lc = [rcopy(mine, mine, lc_s.at[zl], lc_r.at[zl], sibling)]
    for copy in lg + lc:
        copy.start()
    for zz, _ in zpeers:
        ref = lt.at[zz // 2, zz % 2, c]
        rcopy(ref, ref, lg_s.at[0], lg_r.at[zz], sibling).wait_recv()
        copy = rcopy(ref, ref, lc_s.at[zz], lc_r.at[zz], sibling)
        copy.start()
        lc.append(copy)
    for zz in range(4):
        ref = lt.at[zz // 2, zz % 2, 1 - c]
        rcopy(ref, ref, lc_s.at[zz], lc_r.at[zz], sibling).wait_recv()

    p2 = rcopy(p_t.at[:, low, c], p_t.at[:, low, c], p2_s, p2_r, at(zh, x, y, zl + 1 - 2 * low, c))
    p2.start()
    pc = [rcopy(p_t.at[:, low, c], p_t.at[:, low, c], pc_s.at[0], pc_r.at[0], sibling)]
    pc[0].start()

    for t in range(2):
        for u in range(2):
            lt2[2 * t + u] = jnp.concatenate(
                [
                    lt[t, lo, cc, hi * 32 : hi * 32 + 32, u * 256 : u * 256 + 256]
                    for hi in range(2)
                    for lo in range(2)
                    for cc in range(2)
                ],
                axis=0,
            )

    own.wait()
    hs_in = hbuf.at[:, :, pl.ds(pl.multiple_of((1 - c) * 128, 128), 128)]
    rcopy(hs_in, hs_in, hs_s, hs_r, sibling).wait_recv()

    def project(distance):
        rnd, owner = OWNER[distance]
        block = (y + distance) % 8

        @pl.when(x != owner)
        def _():
            ref = hbuf.at[block, :, pl.ds(256, 768)]
            rcopy(ref, ref, hx_s.at[0, 0], hx_r.at[rnd, owner], sibling).wait_recv()

        total = jnp.zeros((224, 256), F32)
        for b in range(4):
            total = total + lax.dot_general(
                hbuf[block, :, b * 256 : b * 256 + 256], lt2[(zl + b) % 4],
                (((1,), (1,)), ((), ())), preferred_element_type=F32,
            )
        part[distance] = total

    def rs_copy(direction, h, step):
        rows = pl.ds(h * 112, 112)
        return rcopy(
            stage.at[direction, step, rows], arrived.at[direction, step, rows],
            rs_s.at[direction, h, step], rs_r.at[direction, h, step], up if direction == 0 else down,
        )

    rs = []

    def rs_send(direction, h, step):
        distance = 4 - step if direction == 0 else 4 + step
        rows = slice(h * 112, h * 112 + 112)
        value = part[distance, rows, :]
        begins = 0 if direction == h else 1
        if step > begins:
            rs_copy(direction, h, step - 1).wait_recv()
            value = value + arrived[direction, step - 1, rows, :].astype(F32)
        stage[direction, step, rows, :] = value.astype(BF)
        copy = rs_copy(direction, h, step)
        copy.start()
        rs.append(copy)

    project(4)
    rs_send(0, 0, 0)
    rs_send(1, 1, 0)
    project(3)
    rs_send(0, 1, 1)
    project(5)
    rs_send(1, 0, 1)
    rs_send(0, 0, 1)
    rs_send(1, 1, 1)
    project(2)
    project(6)
    for direction, h in ((0, 0), (1, 1), (0, 1), (1, 0)):
        rs_send(direction, h, 2)
    project(1)
    project(7)
    for direction, h in ((0, 0), (1, 1), (0, 1), (1, 0)):
        rs_send(direction, h, 3)
    project(0)

    dz, dx = [], []

    def gather_x(h, which, source):
        ref = dr.at[source, pl.ds(h * 112, 112)]
        for k, (_, dev) in enumerate(xpeers):
            copy = rcopy(ref, ref, dx_s.at[h, which, k], dx_r.at[h, source], dev)
            copy.start()
            dx.append(copy)

    for h in (0, 1):
        rows = slice(h * 112, h * 112 + 112)
        value = part[0, rows, :]
        for direction in (0, 1):
            rs_copy(direction, h, 3).wait_recv()
            value = value + arrived[direction, 3, rows, :].astype(F32)
        first_f = 0.9 * m1t[rows, :] + 0.1 * value
        second_f = 0.999 * m2t[rows, :] + 0.001 * value * value
        m1t[rows, :] = first_f
        m2t[rows, :] = second_f
        dr[rank, rows, :] = (first_f / FIRST_FIX / (jnp.sqrt(second_f / SECOND_FIX) + 1e-08)).astype(BF)
        ref = dr.at[rank, pl.ds(h * 112, 112)]
        copy = rcopy(ref, ref, dz_s.at[h], dz_r.at[h], partner)
        copy.start()
        dz.append(copy)
        gather_x(h, 0, rank)

    other = (1 - zh) * 4 + x
    for h in (0, 1):
        ref = dr.at[other, pl.ds(h * 112, 112)]
        rcopy(ref, ref, dz_s.at[h], dz_r.at[h], partner).wait_recv()
        gather_x(h, 1, other)

    ref = p_t.at[:, 1 - low, c]
    rcopy(ref, ref, p2_s, p2_r, sibling).wait_recv()
    pc.append(rcopy(ref, ref, pc_s.at[1], pc_r.at[1], sibling))
    pc[1].start()

    for src, dst in ((m1t, new1), (m2t, new2)):
        pad[...] = jnp.zeros_like(pad)
        pad[:224, :] = src[...]
        dst[...] = pad[...].T[:, :224].astype(BF)

    for k, lo in ((0, low), (1, 1 - low)):
        ref = p_t.at[:, lo, 1 - c]
        rcopy(ref, ref, pc_s.at[k], pc_r.at[k], sibling).wait_recv()
    for h in (0, 1):
        for half in (zh, 1 - zh):
            for sx, _ in xpeers:
                ref = dr.at[half * 4 + sx, pl.ds(h * 112, 112)]
                rcopy(ref, ref, dx_s.at[0, 0, 0], dx_r.at[h, half * 4 + sx], sibling).wait_recv()

    def columns(n, carry):
        lanes = pl.ds(pl.multiple_of(n * 256, 256), 256)
        total = jnp.zeros((224, 256), F32)
        for r in range(8):
            rows = jnp.concatenate(
                [
                    p_t[r, lo, cc, hi * 32 : hi * 32 + 32, lanes]
                    for hi in range(2)
                    for lo in range(2)
                    for cc in range(2)
                ],
                axis=0,
            )
            total = total + jnp.dot(dr[r], rows, preferred_element_type=F32)
        pad[:224, :] = total
        upd[lanes, :] = pad[...].T[:, :224].astype(BF)
        return carry

    lax.fori_loop(0, 4, columns, 0)

    pp.wait_send()
    for copy in ct + hz + hx + [hs, lz] + lg + lc + [p2] + pc + rs + dz + dx:
        copy.wait_send()
    for direction in (0, 1):
        for h in (0, 1):
            for step in range(4 if direction == h else 3):
                ring(direction, h, step).wait_send()
    for k in range(8):

        @pl.when(k % 4 != x)
        def _():
            left_copy(k).wait_send()


def per_device(cotangents, hidden, projector, moment_first, moment_second):
    dma = pltpu.SemaphoreType.DMA
    vmem = pl.BlockSpec(memory_space=pltpu.VMEM)
    return pl.pallas_call(
        body,
        out_shape=(
            jax.ShapeDtypeStruct((1024, 224), BF),
            jax.ShapeDtypeStruct((256, 224), BF),
            jax.ShapeDtypeStruct((256, 224), BF),
        ),
        in_specs=[vmem, pl.BlockSpec(memory_space=pl.ANY), vmem, vmem, vmem],
        out_specs=(vmem, vmem, vmem),
        scratch_shapes=[
            pltpu.VMEM((128, 14336), BF),
            pltpu.VMEM((8, 1792, 128), BF),
            pltpu.VMEM((8, 224, 1024), BF),
            pltpu.VMEM((8, 2, 2, 64, 1024), BF),
            pltpu.VMEM((1024, 512), BF),
            pltpu.VMEM((8, 64, 512), BF),
            pltpu.VMEM((4, 2, 64, 512), BF),
            pltpu.VMEM((64, 512), BF),
            pltpu.VMEM((64, 512), BF),
            pltpu.VMEM((2, 2, 2, 64, 512), BF),
            pltpu.VMEM((4, 256, 256), BF),
            pltpu.VMEM((8, 224, 256), F32),
            pltpu.VMEM((2, 4, 224, 256), BF),
            pltpu.VMEM((2, 4, 224, 256), BF),
            pltpu.VMEM((8, 224, 256), BF),
            pltpu.VMEM((224, 256), F32),
            pltpu.VMEM((224, 256), F32),
            pltpu.VMEM((256, 256), F32),
            dma((2,)),
            dma, dma,
            dma((3,)), dma((3,)),
            dma((2, 2, 4)), dma((2, 2, 4)),
            dma((2, 3, 2)), dma((2, 6)),
            dma((2, 3)), dma((2, 4)),
            dma, dma,
            dma((8,)), dma((4, 2)),
            dma, dma,
            dma((3,)), dma((4,)),
            dma((4,)), dma((4,)),
            dma, dma,
            dma((2,)), dma((2,)),
            dma((2, 2, 4)), dma((2, 2, 4)),
            dma((2,)), dma((2,)),
            dma((2, 2, 3)), dma((2, 8)),
        ],
        compiler_params=pltpu.CompilerParams(
            collective_id=0, has_side_effects=True, vmem_limit_bytes=48 * 2**20
        ),
        cost_estimate=pl.CostEstimate(flops=2_500_000_000, bytes_accessed=6_000_000, transcendentals=60_000),
        name="galore",
    )(cotangents, hidden, projector, moment_first, moment_second)


def solution(mesh):
    return jax.shard_map(
        per_device,
        mesh=mesh,
        in_specs=(
            P("fsdp", "rank"),
            P("fsdp", None),
            P("rank", "fsdp"),
            P("rank", "fsdp"),
            P("rank", "fsdp"),
        ),
        out_specs=(P("rank", "fsdp"), P("rank", "fsdp"), P("rank", "fsdp")),
        check_vma=False,
    )
```

time: 473 us -> 118 us (0.25)
  waiting for transfers between devices: 294 us -> 0 us
  blocking collectives: 144 us -> 0 us
  Pallas kernels: 0 us -> 109 us
  between operations: 13.8 us -> 0.67 us
  matrix products: 11.8 us -> 0 us
    all_gather x2 -> x0, waiting for transfers between devices: 208 us -> none  [the longest x1 129 us: per_device(): proj_rows = lax.all_gather(projector, 'fsdp', axis=1, tiled=True)]
    pallas_call x0 -> x1, Pallas kernels: none -> 109 us  [per_device(): pl.pallas_call(body, out_shape=(jax.ShapeDtypeStruct((1024, 224), BF), ja...]
    all_to_all x1 -> x0, blocking collectives: 102 us -> none  [per_device(): lax.all_to_all(hidden, 'fsdp', split_axis=1, concat_axis=0, tiled=True)]
    reduce_scatter x1 -> x0, waiting for transfers between devices: 85.5 us -> none  [per_device(): lax.psum_scatter(lax.dot_general(columns, cotangents, (((0,), (1,)), ((),...]
    all_gather x1 -> x0, blocking collectives: 42.1 us -> none  [per_device(): lax.all_gather(direction, 'rank', axis=0, tiled=True)]
    dot_general x3 -> x0, matrix products: 11.8 us -> none  [the longest x1 5.63 us: per_device(): jnp.dot(lax.all_gather(left_local, 'fsdp', axis=1, tiled=True), hidden_co...]
  transfers between devices with their start and end apart: 3 -> 0, of which waited for: 3 -> 0; matrix products, arithmetic and copies ran while one was open for 1% -> 0% of each run, Pallas kernels for 0% -> 0%
where the time goes in v1:
time: 118 us
  Pallas kernels  109 us (92%)
  local copies, waits for them, and re-layouts  8.46 us (7%)
    pallas_call x1, Pallas kernels, per_device(): pl.pallas_call(body, out_shape=(jax.ShapeDtypeStruct((1024, 224), BF), ja...  109 us
    unnamed x7, local copies, waits for them, and re-layouts  5.99 us
    pallas_call x3, local copies, waits for them, and re-layouts, per_device(): pl.pallas_call(body, out_shape=(jax.ShapeDtypeStruct((1024, 224), BF), ja...  2.47 us

profile of v1, /device:TPU:1, one launch (start us, length us, event | category | flops | bytes accessed | tf_op | source)
XLA Modules:
  0.0 117.7 jit_solution(3566534357525755528)
XLA Ops:
  0.6 1.0 copy.9.mom1
  1.6 1.0 copy.10.mom2
  2.6 1.0 copy.8.prj
  3.7 0.0 copy-start
  3.7 2.0 %copy-done = bf16[128,14336]{1,0:T(8,128)(2,1)S(1)} copy-done((bf16[128,14336]{1,0:T(8,128)(2,1)S(1)}, bf16[128,14336]{1,0:T(8,128)(2,1)}, u32[]{:S(2)}) %copy-start) | copy-done | bytes 3670040
  5.7 0.0 copy-start.1
  5.7 0.9 copy-done.1
  6.6 108.6 %galore.1 = (bf16[1024,224]{1,0:T(8,128)(2,1)S(1)}, bf16[256,224]{1,0:T(8,128)(2,1)S(1)}, bf16[256,224]{1,0:T(8,128)(2,1)S(1)}) custom-call(bf16[128,1024]{1,0:T(8,128)(2,1)S(1)} %copy-done.1, bf16[128,14336]{1,0:T(8,128)(2,1)S(1)} %copy-done, bf16[1024,32]{1,0:T(8,128)(2,1)S(1)} %copy.8.prj, bf16[256,224]{1,0:T(8,128)(2,1)S(1)} %copy.9.mom1, ...), custom_call_target="tpu_custom_call" | custom-call | flops 2500000000 | bytes 6000000 | tf_op jit(solution)/shard_map/galore/pallas_call | solution.py:425
  115.2 1.0 copy.11
  116.2 0.7 copy.12
  116.9 0.7 copy.13
Async XLA Ops:
  3.7 2.0 %copy-start = (bf16[128,14336]{1,0:T(8,128)(2,1)S(1)}, bf16[128,14336]{1,0:T(8,128)(2,1)}, u32[]{:S(2)}) copy-start(bf16[128,14336]{1,0:T(8,128)(2,1)} %hid.1) | copy-start | bytes 11010052
  5.7 0.9 copy-start.1

commit v2 on v0

v2 whole, which is shorter than its diff:
```python
import jax
import jax.numpy as jnp
from jax import lax
from jax.experimental import pallas as pl
from jax.experimental.pallas import tpu as pltpu
from jax.sharding import PartitionSpec as P

STEP = 20
FIRST_FIX = 1.0 - 0.9**STEP
SECOND_FIX = 1.0 - 0.999**STEP
BF = jnp.bfloat16
F32 = jnp.float32
MESH = pl.DeviceIdType.MESH
OWNER = {4: (0, 0), 3: (0, 1), 5: (0, 2), 2: (0, 3), 0: (1, 0), 7: (1, 1), 1: (1, 2), 6: (1, 3)}
STOP = None
VL = 60
HID = True


def guarded(when, act):
    if when is None:
        act()
    else:
        pl.when(when)(act)


def kernel(*refs):
    state = {"in": {}, "out": [], "local": {}}
    for name in body(state, *refs):
        if name == STOP:
            break
    for copy in list(state["local"].values()):
        copy.wait()
    for copy, when in list(state["in"].values()):
        guarded(when, copy.wait_recv)
    for copy, when in state["out"]:
        guarded(when, copy.wait_send)


def body(
    state, cot, hid, prj, mom1, mom2,
    upd, new1, new2,
    hid_v, cot_v, hid_t, hbuf, p_t, cot_t, xs, xb, zs, zb, lt, part, stage, arrived, dr, m1, m2, n1, n2,
    loc_sem,
    pp_s, pp_r, ct_s, ct_r, ring_s, ring_r, hz_s, hz_r, hx_s, hx_r, hs_s, hs_r,
    ls_s, ls_r, lz_s, lz_r, lg_s, lg_r, lc_s, lc_r, p2_s, p2_r, pc_s, pc_r,
    rs_s, rs_r, dz_s, dz_r, dx_s, dx_r,
):
    inbox, outbox, local = state["in"], state["out"], state["local"]

    def send(copy, when=None):
        guarded(when, copy.start)
        outbox.append((copy, when))

    def expect(key, copy, when=None):
        inbox[key] = (copy, when)

    def receive(key):
        copy, when = inbox.pop(key)
        guarded(when, copy.wait_recv)

    def load(key, copy):
        copy.start()
        local[key] = copy

    def loaded(key):
        local.pop(key).wait()

    rank = lax.axis_index("rank")
    shard = lax.axis_index("fsdp")
    zh, x = rank // 4, rank % 4
    y, zl, c = shard // 8, (shard // 2) % 4, shard % 2
    z = zh * 4 + zl
    low, high = zl % 2, zl // 2

    def at(zh_, x_, y_, zl_, c_):
        return (zh_ * 4 + x_, y_ * 8 + zl_ * 2 + c_)

    def at_z(z_, c_):
        return at(z_ // 4, x, y, z_ % 4, c_)

    def at_y(step, other=False):
        return at(zh, x, (y + step + 8) % 8, (zl + 2) % 4 if other else zl, c)

    def rcopy(src, dst, ssem, rsem, dev):
        return pltpu.make_async_remote_copy(
            src_ref=src, dst_ref=dst, send_sem=ssem, recv_sem=rsem, device_id=dev, device_id_type=MESH
        )

    def landing(ref, sem):
        return rcopy(ref, ref, hs_s, sem, sibling)

    sibling = at(zh, x, y, zl, 1 - c)
    partner = at(1 - zh, x, y, zl, c)
    xpeers = [((x + k) % 4, at(zh, (x + k) % 4, y, zl, c)) for k in (1, 2, 3)]
    zpeers = [((zl + k) % 4, at(zh, x, y, (zl + k) % 4, c)) for k in (1, 2, 3)]

    def shard_ref(block, lo, hi):
        return p_t.at[block, c, lo, pl.ds(pl.multiple_of(hi * 32, 32), 32)]

    yield "start"
    load("prj", pltpu.make_async_copy(prj, shard_ref(y, low, high), loc_sem.at[0]))
    load("cot", pltpu.make_async_copy(cot, cot_v, loc_sem.at[1]))
    load("hid", pltpu.make_async_copy(hid, hid_v, loc_sem.at[2]))
    load("mom1", pltpu.make_async_copy(mom1, m1, loc_sem.at[3]))
    load("mom2", pltpu.make_async_copy(mom2, m2, loc_sem.at[4]))

    barrier = pltpu.get_barrier_semaphore()
    greet = [sibling, partner] + [d for _, d in xpeers] + [d for _, d in zpeers]
    greet += [at_y(1), at_y(-1), at_y(2), at_y(-2), at_y(1, True), at_y(-1, True)]
    greet += [at_z((z + off) % 8, cc) for off in (1, 7, 2, 6) for cc in (0, 1)]
    for dev in greet:
        pl.semaphore_signal(barrier, inc=1, device_id=dev, device_id_type=MESH)

    def cot_ref(lo, cc):
        return cot_t.at[:, pl.ds(pl.multiple_of(lo * 256 + cc * 128, 128), 128)]

    loaded("cot")
    cot_t[:, pl.ds(pl.multiple_of(low * 256 + c * 128, 128), 128)] = cot_v[...].T
    loaded("prj")
    yield "barrier"
    pl.semaphore_wait(barrier, len(greet))
    yield "first_sends"

    def ring_ref(block, kind):
        return shard_ref(block, low, high if kind == 0 else 1 - high)

    def ring_send(direction, kind, step):
        sign = 1 - 2 * direction
        sems = ring_s.at[direction, kind, step], ring_r.at[direction, kind, step]
        origin = (y - sign * min(step, 2) + 8) % 8
        ref = ring_ref(origin, kind)
        send(rcopy(ref, ref, *sems, at_y(sign * (2 if step == 3 else 1))))

    def ring_expect(direction, kind, step):
        origin = (y - (1 - 2 * direction) * (step + 1) + 8) % 8
        expect(("ring", direction, kind, step), landing(ring_ref(origin, kind), ring_r.at[direction, kind, step]))

    own_shard = ring_ref(y, 0)
    for direction in (0, 1):
        sign = 1 - 2 * direction
        for kind in (0, 1):
            send(rcopy(own_shard, own_shard, ring_s.at[direction, kind, 0], ring_r.at[direction, kind, 0],
                       at_y(sign, kind == 1)))
            ring_expect(direction, kind, 0)

    def shard_send(k):
        zz, dev = zpeers[k - 1]
        send(rcopy(own_shard, own_shard, pp_s.at[k], pp_r.at[k], dev))
        source = (zl + 4 - k) % 4
        expect(("pp", k), landing(shard_ref(y, source % 2, source // 2), pp_r.at[k]))

    shard_send(2)

    def cot_send(ref, k, dev):
        send(rcopy(ref, ref, ct_s.at[k], ct_r.at[k], dev))

    cot_send(cot_ref(low, c), 0, at(zh, x, y, zl + 1 - 2 * low, c))
    cot_send(cot_ref(low, c), 1, sibling)
    expect("cot0", landing(cot_ref(1 - low, c), ct_r.at[0]))
    expect("cot1", landing(cot_ref(low, 1 - c), ct_r.at[1]))

    def transpose_block(block):
        def tile(t, carry):
            column = pl.multiple_of(block * 1792 + t * 128, 128)
            row = pl.multiple_of(t * 128, 128)
            hid_t[block, pl.ds(row, 128), :] = hid_v[:, pl.ds(column, 128)].T
            return carry

        lax.fori_loop(0, 14, tile, 0, unroll=7)

    first = jnp.where(x == 0, 4, jnp.where(x == 1, 3, jnp.where(x == 2, 5, 2)))
    blocks = [(y + first) % 8, (y + first + 4) % 8]

    def hidden_send(rnd):
        if not HID:
            return
        block = blocks[rnd]
        for k, (off, rot) in enumerate(((1, 3), (7, 1), (None, 2))):
            zd = (z + off) % 8 if off is not None else (z + 2 + 4 * c) % 8
            lane = pl.multiple_of(rot * 256 + c * 128, 128)
            for cc in (0, 1):
                row = pl.multiple_of((2 * (zd % 4) + cc) * 224, 16)
                send(rcopy(
                    hid_t.at[block, pl.ds(row, 224)], hbuf.at[block, :, pl.ds(lane, 128)],
                    hz_s.at[rnd, k, cc], hz_r.at[rnd, 2 * k + c], at_z(zd, cc),
                ))
                ref = hbuf.at[block, :, pl.ds(rot * 256 + cc * 128, 128)]
                expect(("hz", rnd, k, cc), landing(ref, hz_r.at[rnd, 2 * k + cc]))

    def hidden_forward(rnd):
        if not HID:
            return
        for k in range(3):
            for cc in (0, 1):
                receive(("hz", rnd, k, cc))
        ref = hbuf.at[blocks[rnd], :, pl.ds(256, 768)]
        for k, (_, dev) in enumerate(xpeers):
            send(rcopy(ref, ref, hx_s.at[rnd, k], hx_r.at[rnd, x], dev))
        for distance, (when, owner) in OWNER.items():
            if when == rnd:
                ref = hbuf.at[(y + distance) % 8, :, pl.ds(256, 768)]
                expect(("hx", distance), landing(ref, hx_r.at[rnd, owner]), x != owner)

    yield "hidden_sends"
    loaded("hid")
    for rnd in (0, 1):
        transpose_block(blocks[rnd])
        hidden_send(rnd)
    shard_send(1)
    shard_send(3)

    yield "ring_0"
    for kind in (0, 1):
        for direction in (0, 1):
            receive(("ring", direction, kind, 0))
            ring_send(direction, kind, 1)
            ring_expect(direction, kind, 1)
    for k in range(1, 4):
        transpose_block((blocks[0] + k) % 8)

    yield "ring_1"
    for kind in (0, 1):
        for direction in (0, 1):
            receive(("ring", direction, kind, 1))
            ring_send(direction, kind, 2)
            ring_expect(direction, kind, 2)
            if kind == direction:
                ring_send(direction, kind, 3)
                ring_expect(direction, kind, 3)

    yield "cot_wait"
    receive("cot0")
    cot_send(cot_ref(1 - low, c), 2, sibling)
    expect("cot2", landing(cot_ref(1 - low, 1 - c), ct_r.at[2]))
    for k in range(5, 8):
        transpose_block((blocks[0] + k) % 8)
    hs_lane = pl.ds(pl.multiple_of(c * 128, 128), 128)
    load("own", pltpu.make_async_copy(
        hid_t.at[:, pl.ds(pl.multiple_of((2 * zl + c) * 224, 16), 224)], hbuf.at[:, :, hs_lane], loc_sem.at[5]
    ))
    send(rcopy(
        hid_t.at[:, pl.ds(pl.multiple_of((2 * zl + 1 - c) * 224, 16), 224)], hbuf.at[:, :, hs_lane], hs_s, hs_r, sibling
    ))
    expect("hs", landing(hbuf.at[:, :, pl.ds(pl.multiple_of((1 - c) * 128, 128), 128)], hs_r))
    receive("cot1")
    receive("cot2")
    receive(("pp", 2))

    def left_block(block):
        rows = p_t[block, c, low]
        xs[block] = jnp.dot(rows, cot_t[...], preferred_element_type=F32).astype(BF)
        send(rcopy(
            xs.at[block], xb.at[x, block // 4], ls_s.at[block], ls_r.at[x, block // 4], at(zh, block % 4, y, zl, c)
        ), block % 4 != x)

    yield "left_first"
    for distance in (0, 1, 7, 2, 6):
        left_block((y + distance) % 8)

    yield "ring_2"
    for kind in (0, 1):
        for direction in (0, 1):
            receive(("ring", direction, kind, 2))
    left_block((y + 3) % 8)
    left_block((y + 5) % 8)
    yield "ring_3"
    receive(("ring", 0, 0, 3))
    receive(("ring", 1, 1, 3))
    left_block((y + 4) % 8)

    def rest_send(direction, step):
        sign = 1 - 2 * direction
        origin = (y - sign * min(step, 2) + 8) % 8
        ref = p_t.at[origin, c, 1 - low] if step < 3 else shard_ref(origin, 1 - low, direction)
        send(rcopy(ref, ref, p2_s.at[direction, step], p2_r.at[direction, step], at_y(sign * (2 if step == 3 else 1))))
        origin = (y - sign * (step + 1) + 8) % 8
        ref = p_t.at[origin, c, 1 - low] if step < 3 else shard_ref(origin, 1 - low, direction)
        expect(("p2", direction, step), landing(ref, p2_r.at[direction, step]))

    yield "hidden_forward_0"
    hidden_forward(0)
    yield "rest_0"
    receive(("pp", 1))
    receive(("pp", 3))
    for direction in (0, 1):
        rest_send(direction, 0)

    def left_wait(side):
        for k in range(3):
            receive(("ls", k, side))

    def left_sum(half):
        total = xs[half * 4 + x].astype(F32)
        for sx, _ in xpeers:
            total = total + xb[sx, half].astype(F32)
        return total

    for k, (sx, _) in enumerate(xpeers):
        for side, half in enumerate((zh, 1 - zh)):
            expect(("ls", k, side), landing(xb.at[sx, half], ls_r.at[sx, half]))

    yield "left_x_wait"
    left_wait(1)
    zs[...] = left_sum(1 - zh).astype(BF)
    send(rcopy(zs, zb, lz_s, lz_r, partner))
    expect("lz", landing(zb, lz_r))
    yield "rest_1"
    for direction in (0, 1):
        receive(("p2", direction, 0))
        rest_send(direction, 1)
    left_wait(0)
    yield "left_z_wait"
    receive("lz")
    mine = lt.at[high, c, low]
    lt[high, c, low] = (left_sum(zh) + zb[...].astype(F32)).astype(BF)
    for k, (zz, dev) in enumerate(zpeers):
        send(rcopy(mine, mine, lg_s.at[k], lg_r.at[zl], dev))
        expect(("lg", k), landing(lt.at[zz // 2, c, zz % 2], lg_r.at[zz]))
    send(rcopy(mine, mine, lc_s.at[zl], lc_r.at[zl], sibling))
    for zz in range(4):
        expect(("lc", zz), landing(lt.at[zz // 2, 1 - c, zz % 2], lc_r.at[zz]))
    yield "hidden_forward_1"
    hidden_forward(1)
    yield "rest_2"
    for direction in (0, 1):
        receive(("p2", direction, 1))
        rest_send(direction, 2)
        rest_send(direction, 3)
    yield "left_gather"
    for k, (zz, _) in enumerate(zpeers):
        receive(("lg", k))
        ref = lt.at[zz // 2, c, zz % 2]
        send(rcopy(ref, ref, lc_s.at[zz], lc_r.at[zz], sibling))

    yield "hidden_local"
    loaded("own")
    receive("hs")

    def project(distance, half):
        block = (y + distance) % 8
        if half == 0 and HID:
            receive(("hx", distance))
        cc = c if half == 0 else 1 - c
        total = jnp.zeros((224, 128), F32)
        for b in range(4):
            zz = (zl + b) % 4
            weights = lt[zz // 2, cc, :, :, pl.ds(pl.multiple_of((zz % 2) * 256, 256), 256)].reshape(128, 256)
            total = total + lax.dot_general(
                hbuf[block, :, b * 256 : b * 256 + 256], weights,
                (((1,), (1,)), ((), ())), preferred_element_type=F32,
            )
        part[distance, half] = total

    def sum_copy(direction, half, step):
        sign = 1 - 2 * direction
        return rcopy(
            stage.at[direction, half, step], arrived.at[direction, half, step],
            rs_s.at[direction, half, step], rs_r.at[direction, half, step], at_y(sign * (2 if step == 0 else 1)),
        )

    def sum_send(direction, half, step):
        distance = 4 - step if direction == 0 else 4 + step
        value = part[distance, half]
        sources = [1] + ([0] if half == direction else []) if step == 2 else [2] if step == 3 else []
        for source in sources:
            receive(("sum", direction, half, source))
            value = value + arrived[direction, half, source].astype(F32)
        stage[direction, half, step] = value.astype(BF)
        copy = sum_copy(direction, half, step)
        send(copy)
        expect(("sum", direction, half, step), copy)

    yield "sum_0"
    for half in (0, 1):
        if half == 1:
            for zz in range(4):
                receive(("lc", zz))
        project(4, half)
        sum_send(half, half, 0)
        project(3, half)
        sum_send(0, half, 1)
        project(5, half)
        sum_send(1, half, 1)
    yield "sum_1"
    for half in (0, 1):
        project(2, half)
        project(6, half)
        sum_send(0, half, 2)
        sum_send(1, half, 2)
    yield "rest_3"
    for direction in (0, 1):
        receive(("p2", direction, 2))
        receive(("p2", direction, 3))
    send(rcopy(p_t.at[:, c], p_t.at[:, c], pc_s, pc_r, sibling))
    expect("pc", landing(p_t.at[:, 1 - c], pc_r))
    yield "sum_2"
    for half in (0, 1):
        project(1, half)
        project(7, half)
        sum_send(0, half, 3)
        sum_send(1, half, 3)
    for half in (0, 1):
        project(0, half)

    row = lax.broadcasted_iota(jnp.int32, (256, 256), 0)
    column = lax.broadcasted_iota(jnp.int32, (256, 256), 1)
    swapped = (row // 128) * 32 + ((row // 64) % 2) * 64 + ((row // 32) % 2) * 128 + row % 32
    order = jnp.where(swapped == column, 1.0, 0.0).astype(BF)
    loaded("mom1")
    loaded("mom2")
    n1[...] = jnp.dot(m1[...], order, preferred_element_type=F32)
    n2[...] = jnp.dot(m2[...], order, preferred_element_type=F32)

    def gather_x(half, which, source, lanes):
        ref = dr.at[source, :, lanes]
        for k, (sx, dev) in enumerate(xpeers):
            send(rcopy(ref, ref, dx_s.at[half, which, k], dx_r.at[half, source], dev))
            peer = source - x + sx
            expect(("dx", half, which, k), landing(dr.at[peer, :, lanes], dx_r.at[half, peer]))

    other = (1 - zh) * 4 + x
    lane_sets = []
    for half in (0, 1):
        yield "sum_end_%d" % half
        value = part[0, half]
        for direction in (0, 1):
            receive(("sum", direction, half, 3))
            value = value + arrived[direction, half, 3].astype(F32)
        lanes = pl.ds(pl.multiple_of((c if half == 0 else 1 - c) * 128, 128), 128)
        lane_sets.append(lanes)
        first_f = 0.9 * n1[:, lanes] + 0.1 * value
        second_f = 0.999 * n2[:, lanes] + 0.001 * value * value
        dr[rank, :, lanes] = (first_f / FIRST_FIX / (jnp.sqrt(second_f / SECOND_FIX) + 1e-08)).astype(BF)
        send(rcopy(dr.at[rank, :, lanes], dr.at[rank, :, lanes], dz_s.at[half], dz_r.at[half], partner))
        expect(("dz", half), landing(dr.at[other, :, lanes], dz_r.at[half]))
        gather_x(half, 0, rank, lanes)
        n1[:, lanes] = first_f
        n2[:, lanes] = second_f

    new1[...] = jnp.dot(n1[...].astype(BF), order, preferred_element_type=F32).astype(BF)
    new2[...] = jnp.dot(n2[...].astype(BF), order, preferred_element_type=F32).astype(BF)
    yield "dir_z_wait"
    for half in (0, 1):
        receive(("dz", half))
        gather_x(half, 1, other, lane_sets[half])
    yield "proj_core_wait"
    receive("pc")
    yield "dir_x_wait"
    for which in (0, 1):
        for half in (0, 1):
            for k in range(3):
                receive(("dx", half, which, k))

    yield "update"

    def columns(n, carry):
        lanes = pl.ds(pl.multiple_of(n * 256, 256), 256)
        total = jnp.zeros((224, 256), F32)
        for r in range(8):
            rows = p_t[r, :, :, :, lanes].reshape(256, 256)
            total = total + jnp.dot(dr[r], rows, preferred_element_type=F32)
        upd[:, lanes] = total.astype(BF)
        return carry

    lax.fori_loop(0, 4, columns, 0)


def hand_over(*refs):
    for k in range(3):
        refs[3 + k][...] = refs[k][...]


def per_device(cotangents, hidden, projector, moment_first, moment_second):
    dma = pltpu.SemaphoreType.DMA
    vmem = pl.BlockSpec(memory_space=pltpu.VMEM)
    anywhere = pl.BlockSpec(memory_space=pl.ANY)
    shapes = (
        jax.ShapeDtypeStruct((224, 1024), BF),
        jax.ShapeDtypeStruct((224, 256), BF),
        jax.ShapeDtypeStruct((224, 256), BF),
    )
    results = pl.pallas_call(
        kernel,
        out_shape=shapes,
        in_specs=[pl.BlockSpec(memory_space=pl.ANY)] * 5,
        out_specs=(vmem, vmem, vmem),
        scratch_shapes=[
            pltpu.VMEM((128, 14336), BF),
            pltpu.VMEM((128, 1024), BF),
            pltpu.VMEM((8, 1792, 128), BF),
            pltpu.VMEM((8, 224, 1024), BF),
            pltpu.VMEM((8, 2, 2, 64, 1024), BF),
            pltpu.VMEM((1024, 512), BF),
            pltpu.VMEM((8, 64, 512), BF),
            pltpu.VMEM((4, 2, 64, 512), BF),
            pltpu.VMEM((64, 512), BF),
            pltpu.VMEM((64, 512), BF),
            pltpu.VMEM((2, 2, 2, 64, 512), BF),
            pltpu.VMEM((8, 2, 224, 128), F32),
            pltpu.VMEM((2, 2, 4, 224, 128), BF),
            pltpu.VMEM((2, 2, 4, 224, 128), BF),
            pltpu.VMEM((8, 224, 256), BF),
            pltpu.VMEM((224, 256), BF),
            pltpu.VMEM((224, 256), BF),
            pltpu.VMEM((224, 256), F32),
            pltpu.VMEM((224, 256), F32),
            dma((6,)),
            dma((4,)), dma((4,)),
            dma((3,)), dma((3,)),
            dma((2, 2, 4)), dma((2, 2, 4)),
            dma((2, 3, 2)), dma((2, 6)),
            dma((2, 3)), dma((2, 4)),
            dma, dma,
            dma((8,)), dma((4, 2)),
            dma, dma,
            dma((3,)), dma((4,)),
            dma((4,)), dma((4,)),
            dma((2, 4)), dma((2, 4)),
            dma, dma,
            dma((2, 2, 4)), dma((2, 2, 4)),
            dma((2,)), dma((2,)),
            dma((2, 2, 3)), dma((2, 8)),
        ],
        compiler_params=pltpu.CompilerParams(
            collective_id=0, has_side_effects=True, vmem_limit_bytes=VL * 2**20
        ),
        cost_estimate=pl.CostEstimate(flops=2_500_000_000, bytes_accessed=6_000_000, transcendentals=60_000),
        name="galore",
    )(cotangents, hidden, projector.T, moment_first.T, moment_second.T)
    results = pl.pallas_call(
        hand_over,
        out_shape=shapes,
        in_specs=[vmem] * 3,
        out_specs=(vmem,) * 3,
        cost_estimate=pl.CostEstimate(flops=0, bytes_accessed=1_400_000, transcendentals=0),
        name="hand_over",
    )(*results)
    return tuple(array.T for array in results)


def solution(mesh):
    return jax.shard_map(
        per_device,
        mesh=mesh,
        in_specs=(
            P("fsdp", "rank"),
            P("fsdp", None),
            P("rank", "fsdp"),
            P("rank", "fsdp"),
            P("rank", "fsdp"),
        ),
        out_specs=(P("rank", "fsdp"), P("rank", "fsdp"), P("rank", "fsdp")),
        check_vma=False,
    )
```

time: 473 us -> 94.7 us (0.20)
  the two profiles are of different devices: /device:TPU:1 before, /device:TPU:68 now
where the time goes in v2:
time: 94.7 us; the launch traced here: 94.6 us
  Pallas kernels  93.9 us (99%)
    pallas_call x1, Pallas kernels, per_device(): pl.pallas_call(kernel, out_shape=shapes, in_specs=[pl.BlockSpec(memory_sp...  92 us
    pallas_call x1, Pallas kernels, per_device(): pl.pallas_call(hand_over, out_shape=shapes, in_specs=[vmem] * 3, out_spec...  1.94 us

profile of v2, /device:TPU:68, one launch (start us, length us, event | category | flops | bytes accessed | tf_op | source)
XLA Modules:
  0.0 94.6 jit_solution(4347306204124131687)
XLA Ops:
  0.6 92.0 %galore.1 = (bf16[224,1024]{1,0:T(8,128)(2,1)}, bf16[224,256]{1,0:T(8,128)(2,1)}, bf16[224,256]{1,0:T(8,128)(2,1)}) custom-call(bf16[128,1024]{1,0:T(8,128)(2,1)} %refs_0_.1, bf16[128,14336]{1,0:T(8,128)(2,1)} %refs_1_.1, bf16[32,1024]{1,0:T(8,128)(2,1)} %bitcast.11, bf16[224,256]{1,0:T(8,128)(2,1)} %bitcast.7, bf16[224,256]{1,0:T(8,128)(2,1)} %bitcast.8), custom_call_target="tpu_custom_call" | custom-call | flops 2500000000 | bytes 6000000 | tf_op jit(solution)/shard_map/galore/pallas_call | solution.py:483
  92.6 1.9 %hand_over.1 = (bf16[224,1024]{1,0:T(8,128)(2,1)}, bf16[224,256]{1,0:T(8,128)(2,1)}, bf16[224,256]{1,0:T(8,128)(2,1)}) custom-call(bf16[224,1024]{1,0:T(8,128)(2,1)} %get-tuple-element.9.refs_0_, bf16[224,256]{1,0:T(8,128)(2,1)} %get-tuple-element.10.refs_1_, bf16[224,256]{1,0:T(8,128)(2,1)} %get-tuple-element.11.refs_2_), custom_call_target="tpu_custom_call" | custom-call | bytes 1400000 | tf_op jit(solution)/shard_map/hand_over/pallas_call | solution.py:531

commit v3 on v2

--- a/solution.py
+++ b/solution.py
@@ -11,7 +11,6 @@
 BF = jnp.bfloat16
 F32 = jnp.float32
 MESH = pl.DeviceIdType.MESH
-OWNER = {4: (0, 0), 3: (0, 1), 5: (0, 2), 2: (0, 3), 0: (1, 0), 7: (1, 1), 1: (1, 2), 6: (1, 3)}
 STOP = None
 VL = 60
 HID = True
@@ -40,8 +39,8 @@
 def body(
     state, cot, hid, prj, mom1, mom2,
     upd, new1, new2,
-    hid_v, cot_v, hid_t, hbuf, p_t, cot_t, xs, xb, zs, zb, lt, part, stage, arrived, dr, m1, m2, n1, n2,
-    loc_sem,
+    hid_v, cot_v, hid_t, hbuf, p_t, cot_t, xs, xb, zs, zb, lt, part, stage, arrived, dr, m1, m2, n1, n2, acc, upd_v,
+    loc_sem, out_sem,
     pp_s, pp_r, ct_s, ct_r, ring_s, ring_r, hz_s, hz_r, hx_s, hx_r, hs_s, hs_r,
     ls_s, ls_r, lz_s, lz_r, lg_s, lg_r, lc_s, lc_r, p2_s, p2_r, pc_s, pc_r,
     rs_s, rs_r, dz_s, dz_r, dx_s, dx_r,
@@ -79,8 +78,8 @@
     def at_z(z_, c_):
         return at(z_ // 4, x, y, z_ % 4, c_)
 
-    def at_y(step, other=False):
-        return at(zh, x, (y + step + 8) % 8, (zl + 2) % 4 if other else zl, c)
+    def at_y(step):
+        return at(zh, x, (y + step + 8) % 8, zl, c)
 
     def rcopy(src, dst, ssem, rsem, dev):
         return pltpu.make_async_remote_copy(
@@ -107,7 +106,7 @@
 
     barrier = pltpu.get_barrier_semaphore()
     greet = [sibling, partner] + [d for _, d in xpeers] + [d for _, d in zpeers]
-    greet += [at_y(1), at_y(-1), at_y(2), at_y(-2), at_y(1, True), at_y(-1, True)]
+    greet += [at_y(1), at_y(-1), at_y(2), at_y(-2)]
     greet += [at_z((z + off) % 8, cc) for off in (1, 7, 2, 6) for cc in (0, 1)]
     for dev in greet:
         pl.semaphore_signal(barrier, inc=1, device_id=dev, device_id_type=MESH)
@@ -137,12 +136,6 @@
         expect(("ring", direction, kind, step), landing(ring_ref(origin, kind), ring_r.at[direction, kind, step]))
 
     own_shard = ring_ref(y, 0)
-    for direction in (0, 1):
-        sign = 1 - 2 * direction
-        for kind in (0, 1):
-            send(rcopy(own_shard, own_shard, ring_s.at[direction, kind, 0], ring_r.at[direction, kind, 0],
-                       at_y(sign, kind == 1)))
-            ring_expect(direction, kind, 0)
 
     def shard_send(k):
         zz, dev = zpeers[k - 1]
@@ -151,13 +144,15 @@
         expect(("pp", k), landing(shard_ref(y, source % 2, source // 2), pp_r.at[k]))
 
     shard_send(2)
+    for direction in (0, 1):
+        ring_send(direction, 0, 0)
+        for kind in (0, 1):
+            ring_expect(direction, kind, 0)
 
     def cot_send(ref, k, dev):
         send(rcopy(ref, ref, ct_s.at[k], ct_r.at[k], dev))
 
-    cot_send(cot_ref(low, c), 0, at(zh, x, y, zl + 1 - 2 * low, c))
     cot_send(cot_ref(low, c), 1, sibling)
-    expect("cot0", landing(cot_ref(1 - low, c), ct_r.at[0]))
     expect("cot1", landing(cot_ref(low, 1 - c), ct_r.at[1]))
 
     def transpose_block(block):
@@ -169,8 +164,11 @@
 
         lax.fori_loop(0, 14, tile, 0, unroll=7)
 
-    first = jnp.where(x == 0, 4, jnp.where(x == 1, 3, jnp.where(x == 2, 5, 2)))
-    blocks = [(y + first) % 8, (y + first + 4) % 8]
+    def fetched(position, rnd):
+        first = jnp.where(position == 0, 4, jnp.where(position == 1, 3, jnp.where(position == 2, 5, 2)))
+        return (y + first + 4 * rnd) % 8
+
+    blocks = [fetched(x, rnd) for rnd in (0, 1)]
 
     def hidden_send(rnd):
         if not HID:
@@ -195,46 +193,67 @@
             for cc in (0, 1):
                 receive(("hz", rnd, k, cc))
         ref = hbuf.at[blocks[rnd], :, pl.ds(256, 768)]
-        for k, (_, dev) in enumerate(xpeers):
-            send(rcopy(ref, ref, hx_s.at[rnd, k], hx_r.at[rnd, x], dev))
-        for distance, (when, owner) in OWNER.items():
-            if when == rnd:
-                ref = hbuf.at[(y + distance) % 8, :, pl.ds(256, 768)]
-                expect(("hx", distance), landing(ref, hx_r.at[rnd, owner]), x != owner)
+        for side in (0, 1):
+            send(rcopy(ref, ref, hx_s.at[rnd, side], hx_r.at[rnd, side], xpeers[2 * side][1]))
+            near = fetched((x + 3 + 2 * side) % 4, rnd)
+            expect(("hx", rnd, side), landing(hbuf.at[near, :, pl.ds(256, 768)], hx_r.at[rnd, side]))
+
+    def hidden_further(rnd):
+        if not HID:
+            return
+        far = fetched((x + 2) % 4, rnd)
+        for side in (0, 1):
+            receive(("hx", rnd, side))
+            near = fetched((x + 3 + 2 * side) % 4, rnd)
+            rows = pl.ds(side * 112, 112)
+            ref = hbuf.at[near, rows, pl.ds(256, 768)]
+            send(rcopy(ref, ref, hx_s.at[rnd, 2 + side], hx_r.at[rnd, 2 + side], xpeers[2 * side][1]))
+            expect(("hx", rnd, 2 + side), landing(hbuf.at[far, rows, pl.ds(256, 768)], hx_r.at[rnd, 2 + side]))
+
+    def hidden_wait(rnd):
+        if not HID:
+            return
+        for side in (0, 1):
+            receive(("hx", rnd, 2 + side))
+
+    def ring_pass(direction, kind, step):
+        receive(("ring", direction, kind, step))
+        ring_send(direction, kind, step + 1)
+        ring_expect(direction, kind, step + 1)
+        if step == 1 and kind == direction:
+            ring_send(direction, kind, 3)
+            ring_expect(direction, kind, 3)
 
     yield "hidden_sends"
     loaded("hid")
-    for rnd in (0, 1):
-        transpose_block(blocks[rnd])
-        hidden_send(rnd)
-    shard_send(1)
-    shard_send(3)
-
+    transpose_block(blocks[0])
+    hidden_send(0)
+    transpose_block(blocks[1])
+    yield "pair"
+    cot_send(cot_ref(low, c), 0, at(zh, x, y, zl + 1 - 2 * low, c))
+    expect("cot0", landing(cot_ref(1 - low, c), ct_r.at[0]))
+    receive(("pp", 2))
+    for direction in (0, 1):
+        ring_send(direction, 1, 0)
     yield "ring_0"
-    for kind in (0, 1):
-        for direction in (0, 1):
-            receive(("ring", direction, kind, 0))
-            ring_send(direction, kind, 1)
-            ring_expect(direction, kind, 1)
+    ring_pass(0, 0, 0)
+    ring_pass(1, 0, 0)
     for k in range(1, 4):
         transpose_block((blocks[0] + k) % 8)
-
-    yield "ring_1"
-    for kind in (0, 1):
-        for direction in (0, 1):
-            receive(("ring", direction, kind, 1))
-            ring_send(direction, kind, 2)
-            ring_expect(direction, kind, 2)
-            if kind == direction:
-                ring_send(direction, kind, 3)
-                ring_expect(direction, kind, 3)
-
-    yield "cot_wait"
-    receive("cot0")
-    cot_send(cot_ref(1 - low, c), 2, sibling)
-    expect("cot2", landing(cot_ref(1 - low, 1 - c), ct_r.at[2]))
+    yield "ring_0_1"
+    ring_pass(0, 1, 0)
+    ring_pass(1, 1, 0)
+    ring_pass(0, 0, 1)
+    ring_pass(1, 0, 1)
+    hidden_send(1)
     for k in range(5, 8):
         transpose_block((blocks[0] + k) % 8)
+    yield "hidden_forward_0"
+    hidden_forward(0)
+    yield "ring_1_1"
+    ring_pass(0, 1, 1)
+    ring_pass(1, 1, 1)
+
     hs_lane = pl.ds(pl.multiple_of(c * 128, 128), 128)
     load("own", pltpu.make_async_copy(
         hid_t.at[:, pl.ds(pl.multiple_of((2 * zl + c) * 224, 16), 224)], hbuf.at[:, :, hs_lane], loc_sem.at[5]
@@ -243,9 +262,14 @@
         hid_t.at[:, pl.ds(pl.multiple_of((2 * zl + 1 - c) * 224, 16), 224)], hbuf.at[:, :, hs_lane], hs_s, hs_r, sibling
     ))
     expect("hs", landing(hbuf.at[:, :, pl.ds(pl.multiple_of((1 - c) * 128, 128), 128)], hs_r))
+    yield "cot_wait"
+    receive("cot0")
+    cot_send(cot_ref(1 - low, c), 2, sibling)
+    expect("cot2", landing(cot_ref(1 - low, 1 - c), ct_r.at[2]))
     receive("cot1")
     receive("cot2")
-    receive(("pp", 2))
+    shard_send(1)
+    shard_send(3)
 
     def left_block(block):
         rows = p_t[block, c, low]
@@ -269,22 +293,29 @@
     receive(("ring", 1, 1, 3))
     left_block((y + 4) % 8)
 
-    def rest_send(direction, step):
-        sign = 1 - 2 * direction
-        origin = (y - sign * min(step, 2) + 8) % 8
-        ref = p_t.at[origin, c, 1 - low] if step < 3 else shard_ref(origin, 1 - low, direction)
-        send(rcopy(ref, ref, p2_s.at[direction, step], p2_r.at[direction, step], at_y(sign * (2 if step == 3 else 1))))
-        origin = (y - sign * (step + 1) + 8) % 8
-        ref = p_t.at[origin, c, 1 - low] if step < 3 else shard_ref(origin, 1 - low, direction)
-        expect(("p2", direction, step), landing(ref, p2_r.at[direction, step]))
-
-    yield "hidden_forward_0"
-    hidden_forward(0)
-    yield "rest_0"
-    receive(("pp", 1))
-    receive(("pp", 3))
-    for direction in (0, 1):
-        rest_send(direction, 0)
+    def rest_send_y():
+        for direction in (0, 1):
+            sign = 1 - 2 * direction
+            ref = p_t.at[y, c, 1 - low]
+            send(rcopy(ref, ref, p2_s.at[direction], p2_r.at[direction], at_y(sign)))
+            expect(("p2", direction), landing(p_t.at[(y - sign + 8) % 8, c, 1 - low], p2_r.at[direction]))
+
+    def core_send(k):
+        lo = low if k == 0 else 1 - low
+        ref = p_t.at[:, c, lo]
+        send(rcopy(ref, ref, pc_s.at[k], pc_r.at[k], sibling))
+        expect(("pc", k), landing(p_t.at[:, 1 - c, lo], pc_r.at[k]))
+
+    def rest_send_z():
+        for k in range(2, 7):
+            ref = p_t.at[(y + k) % 8, c, low]
+            send(rcopy(ref, ref, p2_s.at[k], p2_r.at[k], at(zh, x, y, zl + 1 - 2 * low, c)))
+            expect(("p2", k), landing(p_t.at[(y + k) % 8, c, 1 - low], p2_r.at[k]))
+
+    yield "hidden_further_0"
+    hidden_further(0)
+    yield "hidden_forward_1"
+    hidden_forward(1)
 
     def left_wait(side):
         for k in range(3):
@@ -305,10 +336,10 @@
     zs[...] = left_sum(1 - zh).astype(BF)
     send(rcopy(zs, zb, lz_s, lz_r, partner))
     expect("lz", landing(zb, lz_r))
-    yield "rest_1"
-    for direction in (0, 1):
-        receive(("p2", direction, 0))
-        rest_send(direction, 1)
+    yield "rest_0"
+    receive(("pp", 1))
+    receive(("pp", 3))
+    rest_send_y()
     left_wait(0)
     yield "left_z_wait"
     receive("lz")
@@ -318,29 +349,24 @@
         send(rcopy(mine, mine, lg_s.at[k], lg_r.at[zl], dev))
         expect(("lg", k), landing(lt.at[zz // 2, c, zz % 2], lg_r.at[zz]))
     send(rcopy(mine, mine, lc_s.at[zl], lc_r.at[zl], sibling))
-    for zz in range(4):
-        expect(("lc", zz), landing(lt.at[zz // 2, 1 - c, zz % 2], lc_r.at[zz]))
-    yield "hidden_forward_1"
-    hidden_forward(1)
-    yield "rest_2"
-    for direction in (0, 1):
-        receive(("p2", direction, 1))
-        rest_send(direction, 2)
-        rest_send(direction, 3)
+    expect(("lc", 0), landing(lt.at[high, 1 - c, low], lc_r.at[zl]))
+    yield "hidden_further_1"
+    hidden_further(1)
     yield "left_gather"
     for k, (zz, _) in enumerate(zpeers):
         receive(("lg", k))
         ref = lt.at[zz // 2, c, zz % 2]
         send(rcopy(ref, ref, lc_s.at[zz], lc_r.at[zz], sibling))
-
+        expect(("lc", k + 1), landing(lt.at[zz // 2, 1 - c, zz % 2], lc_r.at[zz]))
+
+    rest_send_z()
+    core_send(0)
     yield "hidden_local"
     loaded("own")
     receive("hs")
 
     def project(distance, half):
         block = (y + distance) % 8
-        if half == 0 and HID:
-            receive(("hx", distance))
         cc = c if half == 0 else 1 - c
         total = jnp.zeros((224, 128), F32)
         for b in range(4):
@@ -371,6 +397,8 @@
         send(copy)
         expect(("sum", direction, half, step), copy)
 
+    yield "hidden_wait_0"
+    hidden_wait(0)
     yield "sum_0"
     for half in (0, 1):
         if half == 1:
@@ -382,18 +410,14 @@
         sum_send(0, half, 1)
         project(5, half)
         sum_send(1, half, 1)
+    yield "hidden_wait_1"
+    hidden_wait(1)
     yield "sum_1"
     for half in (0, 1):
         project(2, half)
         project(6, half)
         sum_send(0, half, 2)
         sum_send(1, half, 2)
-    yield "rest_3"
-    for direction in (0, 1):
-        receive(("p2", direction, 2))
-        receive(("p2", direction, 3))
-    send(rcopy(p_t.at[:, c], p_t.at[:, c], pc_s, pc_r, sibling))
-    expect("pc", landing(p_t.at[:, 1 - c], pc_r))
     yield "sum_2"
     for half in (0, 1):
         project(1, half)
@@ -444,26 +468,42 @@
     for half in (0, 1):
         receive(("dz", half))
         gather_x(half, 1, other, lane_sets[half])
-    yield "proj_core_wait"
-    receive("pc")
+    yield "rest"
+    for k in range(7):
+        receive(("p2", k))
+    core_send(1)
+    receive(("pc", 0))
+    receive(("pc", 1))
     yield "dir_x_wait"
-    for which in (0, 1):
+
+    def update(which, finish):
         for half in (0, 1):
             for k in range(3):
                 receive(("dx", half, which, k))
-
-    yield "update"
-
-    def columns(n, carry):
-        lanes = pl.ds(pl.multiple_of(n * 256, 256), 256)
-        total = jnp.zeros((224, 256), F32)
-        for r in range(8):
-            rows = p_t[r, :, :, :, lanes].reshape(256, 256)
-            total = total + jnp.dot(dr[r], rows, preferred_element_type=F32)
-        upd[:, lanes] = total.astype(BF)
-        return carry
-
-    lax.fori_loop(0, 4, columns, 0)
+        begin = (zh if which == 0 else 1 - zh) * 4
+
+        def columns(n, carry):
+            lanes = pl.ds(pl.multiple_of(n * 256, 256), 256)
+            total = acc[n] if finish else jnp.zeros((224, 256), F32)
+            for r in range(4):
+                rows = p_t[begin + r, :, :, :, lanes].reshape(256, 256)
+                total = total + jnp.dot(dr[begin + r], rows, preferred_element_type=F32)
+            if finish:
+                upd_v[:, lanes] = total.astype(BF)
+                pltpu.make_async_copy(upd_v.at[:, lanes], upd.at[:, lanes], out_sem.at[n]).start()
+            else:
+                acc[n] = total
+            return carry
+
+        lax.fori_loop(0, 4, columns, 0)
+
+    yield "update_0"
+    update(0, False)
+    yield "update_1"
+    update(1, True)
+    for n in range(4):
+        lanes = pl.ds(n * 256, 256)
+        pltpu.make_async_copy(upd_v.at[:, lanes], upd.at[:, lanes], out_sem.at[n]).wait()
 
 
 def hand_over(*refs):
@@ -483,8 +523,8 @@
     results = pl.pallas_call(
         kernel,
         out_shape=shapes,
-        in_specs=[pl.BlockSpec(memory_space=pl.ANY)] * 5,
-        out_specs=(vmem, vmem, vmem),
+        in_specs=[anywhere] * 5,
+        out_specs=(anywhere, vmem, vmem),
         scratch_shapes=[
             pltpu.VMEM((128, 14336), BF),
             pltpu.VMEM((128, 1024), BF),
@@ -505,19 +545,22 @@
             pltpu.VMEM((224, 256), BF),
             pltpu.VMEM((224, 256), F32),
             pltpu.VMEM((224, 256), F32),
+            pltpu.VMEM((4, 224, 256), F32),
+            pltpu.VMEM((224, 1024), BF),
             dma((6,)),
+            dma((4,)),
             dma((4,)), dma((4,)),
             dma((3,)), dma((3,)),
             dma((2, 2, 4)), dma((2, 2, 4)),
             dma((2, 3, 2)), dma((2, 6)),
-            dma((2, 3)), dma((2, 4)),
+            dma((2, 4)), dma((2, 4)),
             dma, dma,
             dma((8,)), dma((4, 2)),
             dma, dma,
             dma((3,)), dma((4,)),
             dma((4,)), dma((4,)),
-            dma((2, 4)), dma((2, 4)),
-            dma, dma,
+            dma((7,)), dma((7,)),
+            dma((2,)), dma((2,)),
             dma((2, 2, 4)), dma((2, 2, 4)),
             dma((2,)), dma((2,)),
             dma((2, 2, 3)), dma((2, 8)),

time: 94.7 us -> 85.5 us (0.903)
  the two profiles are of different devices: /device:TPU:68 before, /device:TPU:1 now
where the time goes in v3:
time: 85.5 us; the launch traced here: 84.9 us
  Pallas kernels  84.3 us (99%)
    pallas_call x1, Pallas kernels, per_device(): pl.pallas_call(kernel, out_shape=shapes, in_specs=[anywhere] * 5, out_spe...  82.4 us
    pallas_call x1, Pallas kernels, per_device(): pl.pallas_call(hand_over, out_shape=shapes, in_specs=[vmem] * 3, out_spec...  1.94 us

profile of v3, /device:TPU:1, one launch (start us, length us, event | category | flops | bytes accessed | tf_op | source)
XLA Modules:
  0.0 84.9 jit_solution(2325018375786109821)
XLA Ops:
  0.6 82.4 %galore.1 = (bf16[224,1024]{1,0:T(8,128)(2,1)}, bf16[224,256]{1,0:T(8,128)(2,1)}, bf16[224,256]{1,0:T(8,128)(2,1)}) custom-call(bf16[128,1024]{1,0:T(8,128)(2,1)} %refs_0_.1, bf16[128,14336]{1,0:T(8,128)(2,1)} %refs_1_.1, bf16[32,1024]{1,0:T(8,128)(2,1)} %bitcast.11, bf16[224,256]{1,0:T(8,128)(2,1)} %bitcast.7, bf16[224,256]{1,0:T(8,128)(2,1)} %bitcast.8), custom_call_target="tpu_custom_call" | custom-call | flops 2500000000 | bytes 6000000 | tf_op jit(solution)/shard_map/galore/pallas_call | solution.py:523
  83.0 1.9 %hand_over.1 = (bf16[224,1024]{1,0:T(8,128)(2,1)}, bf16[224,256]{1,0:T(8,128)(2,1)}, bf16[224,256]{1,0:T(8,128)(2,1)}) custom-call(bf16[224,1024]{1,0:T(8,128)(2,1)} %get-tuple-element.9.refs_0_, bf16[224,256]{1,0:T(8,128)(2,1)} %get-tuple-element.10.refs_1_, bf16[224,256]{1,0:T(8,128)(2,1)} %get-tuple-element.11.refs_2_), custom_call_target="tpu_custom_call" | custom-call | bytes 1400000 | tf_op jit(solution)/shard_map/hand_over/pallas_call | solution.py:574

commit v4 on v3

--- a/solution.py
+++ b/solution.py
@@ -13,7 +13,6 @@
 MESH = pl.DeviceIdType.MESH
 STOP = None
 VL = 60
-HID = True
 
 
 def guarded(when, act):
@@ -171,8 +170,6 @@
     blocks = [fetched(x, rnd) for rnd in (0, 1)]
 
     def hidden_send(rnd):
-        if not HID:
-            return
         block = blocks[rnd]
         for k, (off, rot) in enumerate(((1, 3), (7, 1), (None, 2))):
             zd = (z + off) % 8 if off is not None else (z + 2 + 4 * c) % 8
@@ -187,34 +184,33 @@
                 expect(("hz", rnd, k, cc), landing(ref, hz_r.at[rnd, 2 * k + cc]))
 
     def hidden_forward(rnd):
-        if not HID:
-            return
         for k in range(3):
             for cc in (0, 1):
                 receive(("hz", rnd, k, cc))
-        ref = hbuf.at[blocks[rnd], :, pl.ds(256, 768)]
         for side in (0, 1):
-            send(rcopy(ref, ref, hx_s.at[rnd, side], hx_r.at[rnd, side], xpeers[2 * side][1]))
             near = fetched((x + 3 + 2 * side) % 4, rnd)
-            expect(("hx", rnd, side), landing(hbuf.at[near, :, pl.ds(256, 768)], hx_r.at[rnd, side]))
+            for half in (side, 1 - side):
+                rows = pl.ds(half * 112, 112)
+                ref = hbuf.at[blocks[rnd], rows, pl.ds(256, 768)]
+                sems = hx_s.at[rnd, side, half], hx_r.at[rnd, side, half]
+                send(rcopy(ref, ref, *sems, xpeers[2 * side][1]))
+                expect(("hx", rnd, side, half), landing(hbuf.at[near, rows, pl.ds(256, 768)], sems[1]))
 
     def hidden_further(rnd):
-        if not HID:
-            return
         far = fetched((x + 2) % 4, rnd)
         for side in (0, 1):
-            receive(("hx", rnd, side))
+            receive(("hx", rnd, side, side))
             near = fetched((x + 3 + 2 * side) % 4, rnd)
             rows = pl.ds(side * 112, 112)
             ref = hbuf.at[near, rows, pl.ds(256, 768)]
-            send(rcopy(ref, ref, hx_s.at[rnd, 2 + side], hx_r.at[rnd, 2 + side], xpeers[2 * side][1]))
-            expect(("hx", rnd, 2 + side), landing(hbuf.at[far, rows, pl.ds(256, 768)], hx_r.at[rnd, 2 + side]))
+            sems = hx_s.at[rnd, side, 2], hx_r.at[rnd, side, 2]
+            send(rcopy(ref, ref, *sems, xpeers[2 * side][1]))
+            expect(("hx", rnd, side, 2), landing(hbuf.at[far, rows, pl.ds(256, 768)], sems[1]))
 
     def hidden_wait(rnd):
-        if not HID:
-            return
         for side in (0, 1):
-            receive(("hx", rnd, 2 + side))
+            receive(("hx", rnd, side, 1 - side))
+            receive(("hx", rnd, side, 2))
 
     def ring_pass(direction, kind, step):
         receive(("ring", direction, kind, step))
@@ -314,8 +310,6 @@
 
     yield "hidden_further_0"
     hidden_further(0)
-    yield "hidden_forward_1"
-    hidden_forward(1)
 
     def left_wait(side):
         for k in range(3):
@@ -336,6 +330,8 @@
     zs[...] = left_sum(1 - zh).astype(BF)
     send(rcopy(zs, zb, lz_s, lz_r, partner))
     expect("lz", landing(zb, lz_r))
+    yield "hidden_forward_1"
+    hidden_forward(1)
     yield "rest_0"
     receive(("pp", 1))
     receive(("pp", 3))
@@ -462,8 +458,10 @@
         n1[:, lanes] = first_f
         n2[:, lanes] = second_f
 
-    new1[...] = jnp.dot(n1[...].astype(BF), order, preferred_element_type=F32).astype(BF)
-    new2[...] = jnp.dot(n2[...].astype(BF), order, preferred_element_type=F32).astype(BF)
+    m1[...] = jnp.dot(n1[...].astype(BF), order, preferred_element_type=F32).astype(BF)
+    m2[...] = jnp.dot(n2[...].astype(BF), order, preferred_element_type=F32).astype(BF)
+    load("new1", pltpu.make_async_copy(m1, new1, out_sem.at[4]))
+    load("new2", pltpu.make_async_copy(m2, new2, out_sem.at[5]))
     yield "dir_z_wait"
     for half in (0, 1):
         receive(("dz", half))
@@ -507,13 +505,20 @@
 
 
 def hand_over(*refs):
-    for k in range(3):
-        refs[3 + k][...] = refs[k][...]
+    sems = refs[9]
+    reads = [pltpu.make_async_copy(refs[k], refs[6 + k], sems.at[0, k]) for k in range(3)]
+    writes = [pltpu.make_async_copy(refs[6 + k], refs[3 + k], sems.at[1, k]) for k in range(3)]
+    for copy in reads:
+        copy.start()
+    for read, write in zip(reads, writes):
+        read.wait()
+        write.start()
+    for copy in writes:
+        copy.wait()
 
 
 def per_device(cotangents, hidden, projector, moment_first, moment_second):
     dma = pltpu.SemaphoreType.DMA
-    vmem = pl.BlockSpec(memory_space=pltpu.VMEM)
     anywhere = pl.BlockSpec(memory_space=pl.ANY)
     shapes = (
         jax.ShapeDtypeStruct((224, 1024), BF),
@@ -524,7 +529,7 @@
         kernel,
         out_shape=shapes,
         in_specs=[anywhere] * 5,
-        out_specs=(anywhere, vmem, vmem),
+        out_specs=(anywhere, anywhere, anywhere),
         scratch_shapes=[
             pltpu.VMEM((128, 14336), BF),
             pltpu.VMEM((128, 1024), BF),
@@ -548,12 +553,12 @@
             pltpu.VMEM((4, 224, 256), F32),
             pltpu.VMEM((224, 1024), BF),
             dma((6,)),
-            dma((4,)),
+            dma((6,)),
             dma((4,)), dma((4,)),
             dma((3,)), dma((3,)),
             dma((2, 2, 4)), dma((2, 2, 4)),
             dma((2, 3, 2)), dma((2, 6)),
-            dma((2, 4)), dma((2, 4)),
+            dma((2, 2, 3)), dma((2, 2, 3)),
             dma, dma,
             dma((8,)), dma((4, 2)),
             dma, dma,
@@ -574,8 +579,9 @@
     results = pl.pallas_call(
         hand_over,
         out_shape=shapes,
-        in_specs=[vmem] * 3,
-        out_specs=(vmem,) * 3,
+        in_specs=[anywhere] * 3,
+        out_specs=(anywhere,) * 3,
+        scratch_shapes=[pltpu.VMEM(shape.shape, BF) for shape in shapes] + [dma((2, 3))],
         cost_estimate=pl.CostEstimate(flops=0, bytes_accessed=1_400_000, transcendentals=0),
         name="hand_over",
     )(*results)

time: 85.5 us -> 83.4 us (0.975)
  Pallas kernels: 84.3 us -> 82.5 us
    pallas_call x1, Pallas kernels: 82.4 us -> 80.6 us  [per_device(): pl.pallas_call(kernel, out_shape=shapes, in_specs=[anywhere] * 5, out_spe...]
where the time goes in v4:
time: 83.4 us; the launch traced here: 83.1 us
  Pallas kernels  82.5 us (99%)
    pallas_call x1, Pallas kernels, per_device(): pl.pallas_call(kernel, out_shape=shapes, in_specs=[anywhere] * 5, out_spe...  80.6 us
    pallas_call x1, Pallas kernels, per_device(): pl.pallas_call(hand_over, out_shape=shapes, in_specs=[anywhere] * 3, out_...  1.91 us

profile of v4, /device:TPU:1, one launch (start us, length us, event | category | flops | bytes accessed | tf_op | source)
XLA Modules:
  0.0 83.1 jit_solution(3904170884011604631)
XLA Ops:
  0.6 80.6 %galore.1 = (bf16[224,1024]{1,0:T(8,128)(2,1)}, bf16[224,256]{1,0:T(8,128)(2,1)}, bf16[224,256]{1,0:T(8,128)(2,1)}) custom-call(bf16[128,1024]{1,0:T(8,128)(2,1)} %refs_0_.1, bf16[128,14336]{1,0:T(8,128)(2,1)} %refs_1_.1, bf16[32,1024]{1,0:T(8,128)(2,1)} %bitcast.11, bf16[224,256]{1,0:T(8,128)(2,1)} %bitcast.7, bf16[224,256]{1,0:T(8,128)(2,1)} %bitcast.8), custom_call_target="tpu_custom_call" | custom-call | flops 2500000000 | bytes 6000000 | tf_op jit(solution)/shard_map/galore/pallas_call | solution.py:528
  81.2 1.9 %hand_over.1 = (bf16[224,1024]{1,0:T(8,128)(2,1)}, bf16[224,256]{1,0:T(8,128)(2,1)}, bf16[224,256]{1,0:T(8,128)(2,1)}) custom-call(bf16[224,1024]{1,0:T(8,128)(2,1)} %get-tuple-element.9.refs_0_, bf16[224,256]{1,0:T(8,128)(2,1)} %get-tuple-element.10.refs_1_, bf16[224,256]{1,0:T(8,128)(2,1)} %get-tuple-element.11.refs_2_), custom_call_target="tpu_custom_call" | custom-call | bytes 1400000 | tf_op jit(solution)/shard_map/hand_over/pallas_call | solution.py:579

commit v5 on v4

--- a/solution.py
+++ b/solution.py
@@ -356,7 +356,6 @@
         expect(("lc", k + 1), landing(lt.at[zz // 2, 1 - c, zz % 2], lc_r.at[zz]))
 
     rest_send_z()
-    core_send(0)
     yield "hidden_local"
     loaded("own")
     receive("hs")
@@ -414,6 +413,7 @@
         project(6, half)
         sum_send(0, half, 2)
         sum_send(1, half, 2)
+    core_send(0)
     yield "sum_2"
     for half in (0, 1):
         project(1, half)

time: 83.4 us -> 83.4 us (level)
  no operation moved by 1% of the time
where the time goes in v5:
time: 83.4 us; the launch traced here: 83.1 us
  Pallas kernels  82.5 us (99%)
    pallas_call x1, Pallas kernels, per_device(): pl.pallas_call(kernel, out_shape=shapes, in_specs=[anywhere] * 5, out_spe...  80.6 us
    pallas_call x1, Pallas kernels, per_device(): pl.pallas_call(hand_over, out_shape=shapes, in_specs=[anywhere] * 3, out_...  1.91 us

profile of v5, /device:TPU:1, one launch (start us, length us, event | category | flops | bytes accessed | tf_op | source)
XLA Modules:
  0.0 83.1 jit_solution(2519618642925781920)
XLA Ops:
  0.6 80.6 %galore.1 = (bf16[224,1024]{1,0:T(8,128)(2,1)}, bf16[224,256]{1,0:T(8,128)(2,1)}, bf16[224,256]{1,0:T(8,128)(2,1)}) custom-call(bf16[128,1024]{1,0:T(8,128)(2,1)} %refs_0_.1, bf16[128,14336]{1,0:T(8,128)(2,1)} %refs_1_.1, bf16[32,1024]{1,0:T(8,128)(2,1)} %bitcast.11, bf16[224,256]{1,0:T(8,128)(2,1)} %bitcast.7, bf16[224,256]{1,0:T(8,128)(2,1)} %bitcast.8), custom_call_target="tpu_custom_call" | custom-call | flops 2500000000 | bytes 6000000 | tf_op jit(solution)/shard_map/galore/pallas_call | solution.py:528
  81.2 1.9 %hand_over.1 = (bf16[224,1024]{1,0:T(8,128)(2,1)}, bf16[224,256]{1,0:T(8,128)(2,1)}, bf16[224,256]{1,0:T(8,128)(2,1)}) custom-call(bf16[224,1024]{1,0:T(8,128)(2,1)} %get-tuple-element.9.refs_0_, bf16[224,256]{1,0:T(8,128)(2,1)} %get-tuple-element.10.refs_1_, bf16[224,256]{1,0:T(8,128)(2,1)} %get-tuple-element.11.refs_2_), custom_call_target="tpu_custom_call" | custom-call | bytes 1400000 | tf_op jit(solution)/shard_map/hand_over/pallas_call | solution.py:579
